TPU v7x, 32 devices: a whole 2x2x4 slice. The times are simulated.
32 devices in a mesh: grp: 2 (over x), pts: 16 (over z, y, core).
Axes of the slice: x: 2, y: 2, z: 4, core: 2. Of those that a mesh axis runs over, the one named last changes fastest.
Arguments:
- coulomb: bfloat16 [4096, 4096], P('pts'), may hold values from -8 to 8, as said below
- chi_tiles: bfloat16 [16, 12, 5, 256, 256], P('pts', 'grp'), parts along dimension 1, may hold values from -0.0024414062 to 0.0024414062
- tile_offsets: int32 [16, 5], P('pts'), may hold values from -3 to 3, as said below
- tile_counts: int32 [16], P('pts'), may hold values from 1 to 5, as said below
Outputs:
- screened: float32 [4096, 768], P('pts', 'grp'), parts along dimension 1
There are 2 independent parts, one for each index of `grp`. A program takes and returns all parts, laid end to end along the dimension named above; an argument that names none is the same for every part. Nothing has to cross between parts.
Inputs may be any that keep to these rules, and one draw needn't show every extreme that they name: coulomb is symmetric. `tile_offsets`: slots before tile_counts of a tile hold distinct offsets; slots from tile_counts on hold 0 and are ignored; some tile uses all 5 slots and reaches both -3 and 3. `tile_counts`: some tile has 5.
All inputs are finite; a program needn't handle non-finite values.
Results may differ from a plain program's by a relative error of at most 0.0019.
Values may be sent and summed in bfloat16 or wider, within the bound.
A program may use at most 64 MiB of HBM per device.

v0:
```python
import jax
import jax.numpy as jnp
from jax import lax
from jax.sharding import PartitionSpec as P

SLAB = 64
NFREQ = 6
MAXT = 5
REACH = 3


def passed_along(block, axis, distance):
    devices = range(lax.axis_size(axis))
    route = [((i - distance) % len(devices), i) for i in devices]
    return lax.ppermute(block, axis, route)


def shards(coulomb, chi_tiles, tile_offsets, tile_counts):
    own_slab = coulomb[:, :SLAB]
    pieces = []
    for offset in range(-REACH, REACH + 1):
        if offset == 0:
            pieces.append(own_slab)
        else:
            pieces.append(passed_along(own_slab, "pts", -offset))
    stacked = jnp.stack(pieces, axis=0)
    places = jnp.arange(2 * REACH + 1, dtype=jnp.int32)
    slot_ids = jnp.arange(MAXT, dtype=jnp.int32)
    selector = (tile_offsets[0][:, None] + REACH == places[None, :]) & (slot_ids < tile_counts[0])[
        :, None
    ]
    selector = selector.astype(jnp.bfloat16)
    slot_slabs = jnp.einsum(
        "kj,jts->kts", selector, stacked, preferred_element_type=jnp.float32
    ).astype(jnp.bfloat16)
    induced = jnp.einsum(
        "fkab,kbs->afs", chi_tiles[0], slot_slabs, preferred_element_type=jnp.float32
    )
    induced = induced.reshape(induced.shape[0], -1).astype(jnp.bfloat16)
    product = jnp.dot(
        coulomb,
        lax.all_gather(induced, "pts", axis=0, tiled=True),
        preferred_element_type=jnp.float32,
    )
    return jnp.tile(own_slab.astype(jnp.float32), (1, NFREQ)) + product


def solution(mesh):
    return jax.shard_map(
        shards,
        mesh=mesh,
        in_specs=(P("pts", None), P("pts", "grp", None, None, None), P("pts", None), P("pts")),
        out_specs=P("pts", "grp"),
        check_vma=False,
    )
```

profile of v0, /device:TPU:0, one launch (start us, length us, event | category | flops | bytes accessed | tf_op | source)
XLA Modules:
  0.0 86.8 jit_solution(15115008792746570018)
XLA Ops:
  6.5 0.0 copy-start
  6.5 0.0 all-gather.2.cloned.1.call-start
  6.5 1.0 %slice.3 = bf16[256,64]{1,0:T(8,128)(2,1)S(1)} slice(bf16[256,4096]{1,0:T(8,128)(2,1)} %param.4), slice={[0:256], [0:64]} | slice | bytes 65536 | tf_op jit(solution)/shard_map/slice | solution.py:19
  7.5 0.1 copy.12
  7.6 4.5 %collective-permute-start.5 = (bf16[256,64]{0,1:T(8,128)(2,1)S(1)}, bf16[256,64]{0,1:T(8,128)(2,1)S(1)}, u32[]{:S(2)}, u32[]{:S(2)}) collective-permute-start(bf16[256,64]{0,1:T(8,128)(2,1)S(1)} %copy.12), channel_id=1, source_target_pairs={{3,0},{4,1},{5,2},{6,3},{7,4},{8,5},{9,6},{10,7},{11,8},{12,9},{13... | collective-permute-start | bytes 98312 | tf_op jit(solution)/shard_map/ppermute | solution.py:15
  12.2 1.6 %collective-permute-start.4 = (bf16[256,64]{0,1:T(8,128)(2,1)S(1)}, bf16[256,64]{0,1:T(8,128)(2,1)S(1)}, u32[]{:S(2)}, u32[]{:S(2)}) collective-permute-start(bf16[256,64]{0,1:T(8,128)(2,1)S(1)} %copy.12), channel_id=1, source_target_pairs={{2,0},{3,1},{4,2},{5,3},{6,4},{7,5},{8,6},{9,7},{10,8},{11,9},{12,... | collective-permute-start | bytes 98312 | tf_op jit(solution)/shard_map/ppermute | solution.py:15
  13.8 1.3 %collective-permute-start.3 = (bf16[256,64]{0,1:T(8,128)(2,1)S(1)}, bf16[256,64]{0,1:T(8,128)(2,1)S(1)}, u32[]{:S(2)}, u32[]{:S(2)}) collective-permute-start(bf16[256,64]{0,1:T(8,128)(2,1)S(1)} %copy.12), channel_id=1, source_target_pairs={{1,0},{2,1},{3,2},{4,3},{5,4},{6,5},{7,6},{8,7},{9,8},{10,9},{11,1... | collective-permute-start | bytes 98312 | tf_op jit(solution)/shard_map/ppermute | solution.py:15
  15.0 0.0 collective-permute-start.2
  15.0 2.8 %collective-permute-start = (bf16[256,64]{0,1:T(8,128)(2,1)S(1)}, bf16[256,64]{0,1:T(8,128)(2,1)S(1)}, u32[]{:S(2)}, u32[]{:S(2)}) collective-permute-start(bf16[256,64]{0,1:T(8,128)(2,1)S(1)} %copy.12), channel_id=1, source_target_pairs={{13,0},{14,1},{15,2},{0,3},{1,4},{2,5},{3,6},{4,7},{5,8},{6,9},{7,... | collective-permute-start | bytes 98312 | tf_op jit(solution)/shard_map/ppermute | solution.py:15
  18.5 0.7 add_bitcast_fusion
  19.1 1.1 %collective-permute-done = bf16[256,64]{0,1:T(8,128)(2,1)S(1)} collective-permute-done((bf16[256,64]{0,1:T(8,128)(2,1)S(1)}, bf16[256,64]{0,1:T(8,128)(2,1)S(1)}, u32[]{:S(2)}, u32[]{:S(2)}) %collective-permute-start) | collective-permute-done | bytes 32800 | tf_op jit(solution)/shard_map/ppermute | solution.py:15
  20.2 1.8 %collective-permute-start.1 = (bf16[256,64]{0,1:T(8,128)(2,1)S(1)}, bf16[256,64]{0,1:T(8,128)(2,1)S(1)}, u32[]{:S(2)}, u32[]{:S(2)}) collective-permute-start(bf16[256,64]{0,1:T(8,128)(2,1)S(1)} %copy.12), channel_id=1, source_target_pairs={{14,0},{15,1},{0,2},{1,3},{2,4},{3,5},{4,6},{5,7},{6,8},{7,9},{8,1... | collective-permute-start | bytes 98312 | tf_op jit(solution)/shard_map/ppermute | solution.py:15
  22.0 4.8 %collective-permute-done.1 = bf16[256,64]{0,1:T(8,128)(2,1)S(1)} collective-permute-done((bf16[256,64]{0,1:T(8,128)(2,1)S(1)}, bf16[256,64]{0,1:T(8,128)(2,1)S(1)}, u32[]{:S(2)}, u32[]{:S(2)}) %collective-permute-start.1) | collective-permute-done | bytes 32800 | tf_op jit(solution)/shard_map/ppermute | solution.py:15
  26.8 0.0 collective-permute-done.2
  26.8 0.0 collective-permute-done.3
  26.8 0.0 collective-permute-done.4
  26.9 0.0 collective-permute-done.5
  26.9 0.3 fusion.9
  27.2 4.1 %fusion.6 = bf16[64,6,256]{2,0,1:T(8,128)(2,1)} fusion(bf16[1,6,5,256,256]{4,3,2,1,0:T(8,128)(2,1)} %param.5, bf16[5,256,64]{1,0,2:T(8,128)(2,1)S(1)} %fusion.9), kind=kOutput, calls=%fused_computation.5 | convolution fusion | flops 251756544 | bytes 4292608 | tf_op jit(solution)/shard_map/fkab,kbs->afs/dot_general | solution.py:36
  31.3 0.0 all-gather.2.cloned.1.call-update
  31.3 44.8 %all-gather.2.cloned.1.call-done = bf16[4096,384]{0,1:T(8,128)(2,1)} async-done(((bf16[256,384]{0,1:T(8,128)(2,1)}), bf16[4096,384]{0,1:T(8,128)(2,1)}) %all-gather.2.cloned.1.call-update) | async-done | bytes 3145744 | tf_op jit(solution)/shard_map/all_gather | solution.py:42
  76.1 0.0 copy-done
  76.1 2.9 %fusion.5 = f32[256,384]{0,1:T(8,128)S(1)} fusion(f32[256,384]{0,1:T(8,128)S(1)} %bitcast.47, bf16[4096,384]{0,1:T(8,128)(2,1)} %all-gather.2.cloned.1.call-done, bf16[256,4096]{1,0:T(8,128)(2,1)S(1)} %copy-done), kind=kOutput, calls=%fused_computation.4 | convolution fusion | flops 805404672 | bytes 6029312 | tf_op jit(solution)/shard_map/dot_general | solution.py:40
  79.0 0.9 %copy.8 = f32[256,384]{1,0:T(8,128)} copy(f32[256,384]{0,1:T(8,128)S(1)} %fusion.5) | data formatting | bytes 786432 | tf_op jit(solution)/shard_map/add | solution.py:45
  (9 shorter events, 0.1 us)
Async XLA Ops:
  6.5 69.5 %copy-start = (bf16[256,4096]{1,0:T(8,128)(2,1)S(1)}, bf16[256,4096]{1,0:T(8,128)(2,1)}, u32[]{:S(2)}) copy-start(bf16[256,4096]{1,0:T(8,128)(2,1)} %param.4) | copy-start | bytes 6291460
  6.5 69.5 %all-gather.2.cloned.1.call-start = ((), (), s32[]{:S(2)}) async-start(), calls=%async_computation | async-start | bytes 3342336 | tf_op jit(solution)/shard_map/all_gather | solution.py:42
  7.6 19.2 %collective-permute-start.5 = (bf16[256,64]{0,1:T(8,128)(2,1)S(1)}, bf16[256,64]{0,1:T(8,128)(2,1)S(1)}, u32[]{:S(2)}, u32[]{:S(2)}) collective-permute-start(bf16[256,64]{0,1:T(8,128)(2,1)S(1)} %copy.12), channel_id=1, source_target_pairs={{3,0},{4,1},{5,2},{6,3},{7,4},{8,5},{9,6},{10,7},{11,8},{12,9},{13... | collective-permute-start | bytes 98312 | tf_op jit(solution)/shard_map/ppermute | solution.py:15
  12.2 14.7 %collective-permute-start.4 = (bf16[256,64]{0,1:T(8,128)(2,1)S(1)}, bf16[256,64]{0,1:T(8,128)(2,1)S(1)}, u32[]{:S(2)}, u32[]{:S(2)}) collective-permute-start(bf16[256,64]{0,1:T(8,128)(2,1)S(1)} %copy.12), channel_id=1, source_target_pairs={{2,0},{3,1},{4,2},{5,3},{6,4},{7,5},{8,6},{9,7},{10,8},{11,9},{12,... | collective-permute-start | bytes 98312 | tf_op jit(solution)/shard_map/ppermute | solution.py:15
  13.8 13.1 %collective-permute-start.3 = (bf16[256,64]{0,1:T(8,128)(2,1)S(1)}, bf16[256,64]{0,1:T(8,128)(2,1)S(1)}, u32[]{:S(2)}, u32[]{:S(2)}) collective-permute-start(bf16[256,64]{0,1:T(8,128)(2,1)S(1)} %copy.12), channel_id=1, source_target_pairs={{1,0},{2,1},{3,2},{4,3},{5,4},{6,5},{7,6},{8,7},{9,8},{10,9},{11,1... | collective-permute-start | bytes 98312 | tf_op jit(solution)/shard_map/ppermute | solution.py:15
  15.0 11.8 %collective-permute-start.2 = (bf16[256,64]{0,1:T(8,128)(2,1)S(1)}, bf16[256,64]{0,1:T(8,128)(2,1)S(1)}, u32[]{:S(2)}, u32[]{:S(2)}) collective-permute-start(bf16[256,64]{0,1:T(8,128)(2,1)S(1)} %copy.12), channel_id=1, source_target_pairs={{15,0},{0,1},{1,2},{2,3},{3,4},{4,5},{5,6},{6,7},{7,8},{8,9},{9,10... | collective-permute-start | bytes 98312 | tf_op jit(solution)/shard_map/ppermute | solution.py:15
  15.0 5.1 %collective-permute-start = (bf16[256,64]{0,1:T(8,128)(2,1)S(1)}, bf16[256,64]{0,1:T(8,128)(2,1)S(1)}, u32[]{:S(2)}, u32[]{:S(2)}) collective-permute-start(bf16[256,64]{0,1:T(8,128)(2,1)S(1)} %copy.12), channel_id=1, source_target_pairs={{13,0},{14,1},{15,2},{0,3},{1,4},{2,5},{3,6},{4,7},{5,8},{6,9},{7,... | collective-permute-start | bytes 98312 | tf_op jit(solution)/shard_map/ppermute | solution.py:15
  20.2 6.6 %collective-permute-start.1 = (bf16[256,64]{0,1:T(8,128)(2,1)S(1)}, bf16[256,64]{0,1:T(8,128)(2,1)S(1)}, u32[]{:S(2)}, u32[]{:S(2)}) collective-permute-start(bf16[256,64]{0,1:T(8,128)(2,1)S(1)} %copy.12), channel_id=1, source_target_pairs={{14,0},{15,1},{0,2},{1,3},{2,4},{3,5},{4,6},{5,7},{6,8},{7,9},{8,1... | collective-permute-start | bytes 98312 | tf_op jit(solution)/shard_map/ppermute | solution.py:15
Sparse Core Ops, SparseCore 0:
  31.4 44.5 all-gather.1
where the time goes:
time: 87 us; the launch traced here: 86.8 us
  waiting for transfers between devices  50.6 us (58%)
  between operations  14.1 us (16%)
  starting transfers between devices  12 us (14%)
  matrix products  7.27 us (8%)
  local copies, waits for them, and re-layouts  2.06 us (2%)
    all_gather x1, waiting for transfers between devices, shards(): lax.all_gather(induced, 'pts', axis=0, tiled=True)  44.8 us
    ppermute x6, starting transfers between devices, passed_along(): return lax.ppermute(block, axis, route)  12 us
    ppermute x6, waiting for transfers between devices, passed_along(): return lax.ppermute(block, axis, route)  5.87 us
    dot_general x1, matrix products, shards(): jnp.einsum('fkab,kbs->afs', chi_tiles[0], slot_slabs, preferred_element_t...  4.09 us
    dot_general x1, matrix products, shards(): jnp.dot(coulomb, lax.all_gather(induced, 'pts', axis=0, tiled=True), pref...  2.9 us
  transfers between devices with their start and end apart: 7, of which 3 were waited for; matrix products, arithmetic and copies ran while one was open for 1% of the time, Pallas kernels for 0%

commit v1 on v0

v1 whole, which is shorter than its diff:
```python
import functools

import jax
import jax.numpy as jnp
from jax import lax
from jax.experimental import pallas as pl
from jax.experimental.pallas import tpu as pltpu
from jax.sharding import PartitionSpec as P

SLAB = 64
REACH = 3
MESH = pl.DeviceIdType.MESH


def kernel(
    n, offsets_ref, counts_ref, coulomb_hbm, chi_hbm, out_ref,
    coulomb, chi, slabs, gathered,
    local_sem, halo_send, halo_recv, ring_send, ring_recv, sib_send, sib_recv,
):
    tile = coulomb.shape[0]
    nfreq, maxt = chi.shape[:2]
    chunks = gathered.shape[1]
    per = nfreq // chunks
    wide = per * SLAB
    chips = n // 2
    cols = 2 if n == 16 else 1
    height = chips // cols
    me = lax.axis_index("pts")
    core = me % 2
    sib = me + 1 - 2 * core
    chip = me // 2
    col = chip % cols
    up = chip // cols
    pos = col * height + up + col * (height - 1 - 2 * up)
    way = 1 - 2 * core

    def device_at(place, core):
        place = (place + 2 * chips) % chips
        col = place // height
        up = place % height
        return ((up + col * (height - 1 - 2 * up)) * cols + col) * 2 + core

    ring_to = device_at(pos + way, core)
    ring_from = device_at(pos - way, core)

    head = 128
    first = pltpu.make_async_copy(
        coulomb_hbm.at[:, pl.ds(0, head)], coulomb.at[:, pl.ds(0, head)], local_sem.at[0]
    )
    rest = pltpu.make_async_copy(
        coulomb_hbm.at[:, pl.ds(head, coulomb.shape[1] - head)],
        coulomb.at[:, pl.ds(head, coulomb.shape[1] - head)],
        local_sem.at[1],
    )
    chi_copies = [
        pltpu.make_async_copy(
            chi_hbm.at[0, pl.ds(j * per, per)], chi.at[pl.ds(j * per, per)], local_sem.at[2 + j]
        )
        for j in range(chunks)
    ]
    first.start()
    for c in chi_copies:
        c.start()
    rest.start()

    barrier = pltpu.get_barrier_semaphore()
    others = [d for d in range(-REACH, REACH + 1) if d != 0]
    for d in others:
        pl.semaphore_signal(
            barrier, inc=1, device_id={"pts": (me + d + n) % n}, device_id_type=MESH
        )
    for peer in (ring_to, ring_from):
        pl.semaphore_signal(barrier, inc=1, device_id={"pts": peer}, device_id_type=MESH)

    first.wait()
    own = coulomb[:, :SLAB]
    slabs[REACH] = own.astype(jnp.float32).T.astype(jnp.bfloat16)
    start = own.astype(jnp.float32)
    out_ref[...] = jnp.concatenate([start] * nfreq, axis=1)

    pl.semaphore_wait(barrier, len(others) + 2)

    def halo(d):
        return pltpu.make_async_remote_copy(
            src_ref=slabs.at[REACH],
            dst_ref=slabs.at[REACH - d],
            send_sem=halo_send.at[REACH + d],
            recv_sem=halo_recv.at[REACH - d],
            device_id={"pts": (me + d + n) % n},
            device_id_type=MESH,
        )

    for d in sorted(others, key=abs, reverse=True):
        halo(d).start()

    def to_ring(step, owner, j):
        return pltpu.make_async_remote_copy(
            src_ref=gathered.at[owner, j],
            dst_ref=gathered.at[owner, j],
            send_sem=ring_send.at[step, j],
            recv_sem=ring_recv.at[step, j],
            device_id={"pts": ring_to},
            device_id_type=MESH,
        )

    def to_sib(step, owner, j):
        return pltpu.make_async_remote_copy(
            src_ref=gathered.at[owner, j],
            dst_ref=gathered.at[owner, j],
            send_sem=sib_send.at[step, j],
            recv_sem=sib_recv.at[step, j],
            device_id={"pts": sib},
            device_id_type=MESH,
        )

    for d in others:
        halo(d).wait_recv()

    count = counts_ref[0]
    picked = []
    for k in range(maxt):
        slab = slabs[offsets_ref[0, k] + REACH]
        picked.append(jnp.where(k < count, slab, jnp.zeros_like(slab)))
    for j in range(chunks):
        chi_copies[j].wait()
        parts = []
        for f in range(j * per, (j + 1) * per):
            total = None
            for k in range(maxt):
                term = lax.dot_general(
                    chi[f, k], picked[k], (((1,), (1,)), ((), ())),
                    preferred_element_type=jnp.float32,
                )
                total = term if total is None else total + term
            parts.append(total)
        gathered[me, j] = jnp.concatenate(parts, axis=1).astype(jnp.bfloat16)
        to_ring(0, me, j).start()
        to_sib(0, me, j).start()

    rest.wait()

    def product(owner, j):
        columns = pl.ds(pl.multiple_of(owner * tile, tile), tile)
        return jnp.dot(coulomb[:, columns], gathered[owner, j], preferred_element_type=jnp.float32)

    for j in range(chunks):
        out_ref[:, j * wide : (j + 1) * wide] += product(me, j)

    def turn(step, carry):
        owner = device_at(pos - step * way, core)
        sib_owner = device_at(pos + (step - 1) * way, 1 - core)
        for j in range(chunks):
            to_ring(step - 1, owner, j).wait_recv()

            @pl.when(step < chips - 1)
            def _():
                to_ring(step, owner, j).start()

            to_sib(step, owner, j).start()
            to_sib(step - 1, sib_owner, j).wait_recv()
            out_ref[:, j * wide : (j + 1) * wide] += product(owner, j) + product(sib_owner, j)
        return carry

    lax.fori_loop(1, chips, turn, 0)

    last = device_at(pos + (chips - 1) * way, 1 - core)
    for j in range(chunks):
        to_sib(chips - 1, last, j).wait_recv()
        out_ref[:, j * wide : (j + 1) * wide] += product(last, j)

    for d in others:
        halo(d).wait_send()

    def settle(step, carry):
        for j in range(chunks):
            to_sib(step, me, j).wait_send()

            @pl.when(step < chips - 1)
            def _():
                to_ring(step, me, j).wait_send()
        return carry

    lax.fori_loop(0, chips, settle, 0)


def shards(n, coulomb, chi_tiles, tile_offsets, tile_counts):
    tile, points = coulomb.shape
    _, nfreq, maxt = chi_tiles.shape[:3]
    chunks = nfreq // 2
    chips = n // 2
    return pl.pallas_call(
        functools.partial(kernel, n),
        out_shape=jax.ShapeDtypeStruct((tile, nfreq * SLAB), jnp.float32),
        in_specs=[
            pl.BlockSpec(memory_space=pltpu.SMEM),
            pl.BlockSpec(memory_space=pltpu.SMEM),
            pl.BlockSpec(memory_space=pl.ANY),
            pl.BlockSpec(memory_space=pl.ANY),
        ],
        out_specs=pl.BlockSpec(memory_space=pltpu.VMEM),
        scratch_shapes=[
            pltpu.VMEM((tile, points), jnp.bfloat16),
            pltpu.VMEM(chi_tiles.shape[1:], jnp.bfloat16),
            pltpu.VMEM((2 * REACH + 1, SLAB, tile), jnp.bfloat16),
            pltpu.VMEM((n, chunks, tile, 2 * SLAB), jnp.bfloat16),
            pltpu.SemaphoreType.DMA((2 + chunks,)),
            pltpu.SemaphoreType.DMA((2 * REACH + 1,)),
            pltpu.SemaphoreType.DMA((2 * REACH + 1,)),
            pltpu.SemaphoreType.DMA((chips, chunks)),
            pltpu.SemaphoreType.DMA((chips, chunks)),
            pltpu.SemaphoreType.DMA((chips, chunks)),
            pltpu.SemaphoreType.DMA((chips, chunks)),
        ],
        compiler_params=pltpu.CompilerParams(
            collective_id=0, has_side_effects=True, vmem_limit_bytes=48 * 1024 * 1024
        ),
        cost_estimate=pl.CostEstimate(
            flops=2 * tile * points * nfreq * SLAB, bytes_accessed=6 * 1024 * 1024, transcendentals=0
        ),
    )(tile_offsets, tile_counts, coulomb, chi_tiles)


def solution(mesh):
    return jax.shard_map(
        functools.partial(shards, mesh.shape["pts"]),
        mesh=mesh,
        in_specs=(P("pts", None), P("pts", "grp", None, None, None), P("pts", None), P("pts")),
        out_specs=P("pts", "grp"),
        check_vma=False,
    )
```

time: 87 us -> 40.6 us (0.47)
  waiting for transfers between devices: 50.6 us -> 0 us
  Pallas kernels: 0 us -> 36.6 us
  between operations: 14.1 us -> 0.67 us
  starting transfers between devices: 12 us -> 0 us
  matrix products: 7.27 us -> 0 us
  local copies, waits for them, and re-layouts: 2.06 us -> 2.99 us
    all_gather x1 -> x0, waiting for transfers between devices: 44.8 us -> none  [shards(): lax.all_gather(induced, 'pts', axis=0, tiled=True)]
    pallas_call x0 -> x1, Pallas kernels: none -> 36.6 us  [shards(): pl.pallas_call(functools.partial(kernel, n), out_shape=jax.ShapeDtypeStru...]
    ppermute x6 -> x0, starting transfers between devices: 12 us -> none  [passed_along(): return lax.ppermute(block, axis, route)]
    dot_general x3 -> x0, matrix products: 7.27 us -> none  [the longest x1 4.09 us: shards(): jnp.einsum('fkab,kbs->afs', chi_tiles[0], slot_slabs, preferred_element_t...]
    ppermute x6 -> x0, waiting for transfers between devices: 5.87 us -> none  [passed_along(): return lax.ppermute(block, axis, route)]
    unnamed x9 -> x5, local copies, waits for them, and re-layouts: 0.12 us -> 2.99 us
    slice x1 -> x0, local copies, waits for them, and re-layouts: 0.99 us -> none  [shards(): own_slab = coulomb[:, :SLAB]]
    add x1 -> x0, local copies, waits for them, and re-layouts: 0.91 us -> none  [shards(): return jnp.tile(own_slab.astype(jnp.float32), (1, NFREQ)) + product]
  transfers between devices with their start and end apart: 7 -> 0, of which waited for: 3 -> 0; matrix products, arithmetic and copies ran while one was open for 1% -> 0% of each run, Pallas kernels for 0% -> 0%
where the time goes in v1:
time: 40.6 us; the launch traced here: 40.3 us
  Pallas kernels  36.6 us (90%)
  local copies, waits for them, and re-layouts  2.99 us (7%)
  between operations  0.67 us (2%)
    pallas_call x1, Pallas kernels, shards(): pl.pallas_call(functools.partial(kernel, n), out_shape=jax.ShapeDtypeStru...  36.6 us
    unnamed x5, local copies, waits for them, and re-layouts  2.99 us

profile of v1, /device:TPU:0, one launch (start us, length us, event | category | flops | bytes accessed | tf_op | source)
XLA Modules:
  0.0 40.3 jit_solution(5057139963892669594)
XLA Ops:
  0.7 0.0 copy-start
  0.7 1.6 %copy-done = bf16[256,4096]{1,0:T(8,128)(2,1)S(1)} copy-done((bf16[256,4096]{1,0:T(8,128)(2,1)S(1)}, bf16[256,4096]{1,0:T(8,128)(2,1)}, u32[]{:S(2)}) %copy-start) | copy-done | bytes 2097176
  2.2 0.0 copy-start.1
  2.2 0.7 %copy-done.1 = s32[1,5]{1,0:T(1,128)S(1)} copy-done((s32[1,5]{1,0:T(1,128)S(1)}, s32[1,5]{1,0:T(1,128)}, u32[]{:S(2)}) %copy-start.1) | copy-done | bytes 44
  2.9 36.6 %shard_map.46 = f32[256,384]{1,0:T(8,128)S(1)} custom-call(s32[1,5]{1,0:T(1,128)S(1)} %copy-done.1, s32[1]{0:T(128)S(6)} %copy.6.counts_ref, bf16[256,4096]{1,0:T(8,128)(2,1)S(1)} %copy-done, bf16[1,6,5,256,256]{4,3,2,1,0:T(8,128)(2,1)} %chi_hbm.1), custom_call_target="tpu_custom_call" | custom-call | flops 805306368 | bytes 6291456 | tf_op jit(solution)/shard_map/pallas_call | solution.py:191
  39.5 0.7 %copy.7 = f32[256,384]{1,0:T(8,128)} copy(f32[256,384]{1,0:T(8,128)S(1)} %shard_map.46) | data formatting | bytes 786432
Async XLA Ops:
  0.7 1.6 %copy-start = (bf16[256,4096]{1,0:T(8,128)(2,1)S(1)}, bf16[256,4096]{1,0:T(8,128)(2,1)}, u32[]{:S(2)}) copy-start(bf16[256,4096]{1,0:T(8,128)(2,1)} %coulomb_hbm.1) | copy-start | bytes 6291460
  2.2 0.7 %copy-start.1 = (s32[1,5]{1,0:T(1,128)S(1)}, s32[1,5]{1,0:T(1,128)}, u32[]{:S(2)}) copy-start(s32[1,5]{1,0:T(1,128)} %offsets_ref.1) | copy-start | bytes 64

commit v2 on v1

--- a/solution.py
+++ b/solution.py
@@ -13,8 +13,8 @@
 
 
 def kernel(
-    n, offsets_ref, counts_ref, coulomb_hbm, chi_hbm, out_ref,
-    coulomb, chi, slabs, gathered,
+    n, offsets_hbm, counts_hbm, coulomb_hbm, chi_hbm, out_ref,
+    offsets_ref, counts_ref, coulomb, chi, slabs, gathered,
     local_sem, halo_send, halo_recv, ring_send, ring_recv, sib_send, sib_recv,
 ):
     tile = coulomb.shape[0]
@@ -58,7 +58,13 @@
         )
         for j in range(chunks)
     ]
+    table_copies = [
+        pltpu.make_async_copy(offsets_hbm, offsets_ref, local_sem.at[2 + chunks]),
+        pltpu.make_async_copy(counts_hbm, counts_ref, local_sem.at[3 + chunks]),
+    ]
     first.start()
+    for c in table_copies:
+        c.start()
     for c in chi_copies:
         c.start()
     rest.start()
@@ -93,22 +99,22 @@
     for d in sorted(others, key=abs, reverse=True):
         halo(d).start()
 
-    def to_ring(step, owner, j):
+    def to_ring(stream, step, owner, j):
         return pltpu.make_async_remote_copy(
             src_ref=gathered.at[owner, j],
             dst_ref=gathered.at[owner, j],
-            send_sem=ring_send.at[step, j],
-            recv_sem=ring_recv.at[step, j],
-            device_id={"pts": ring_to},
+            send_sem=ring_send.at[stream, step, j],
+            recv_sem=ring_recv.at[stream, step, j],
+            device_id={"pts": ring_to if stream == 0 else ring_from},
             device_id_type=MESH,
         )
 
-    def to_sib(step, owner, j):
+    def to_sib(stream, step, owner, j):
         return pltpu.make_async_remote_copy(
             src_ref=gathered.at[owner, j],
             dst_ref=gathered.at[owner, j],
-            send_sem=sib_send.at[step, j],
-            recv_sem=sib_recv.at[step, j],
+            send_sem=sib_send.at[stream, step, j],
+            recv_sem=sib_recv.at[stream, step, j],
             device_id={"pts": sib},
             device_id_type=MESH,
         )
@@ -116,6 +122,8 @@
     for d in others:
         halo(d).wait_recv()
 
+    for c in table_copies:
+        c.wait()
     count = counts_ref[0]
     picked = []
     for k in range(maxt):
@@ -134,8 +142,9 @@
                 total = term if total is None else total + term
             parts.append(total)
         gathered[me, j] = jnp.concatenate(parts, axis=1).astype(jnp.bfloat16)
-        to_ring(0, me, j).start()
-        to_sib(0, me, j).start()
+        to_ring(0, 0, me, j).start()
+        to_ring(1, 0, me, j).start()
+        to_sib(0, 0, me, j).start()
 
     rest.wait()
 
@@ -146,41 +155,69 @@
     for j in range(chunks):
         out_ref[:, j * wide : (j + 1) * wide] += product(me, j)
 
-    def turn(step, carry):
-        owner = device_at(pos - step * way, core)
-        sib_owner = device_at(pos + (step - 1) * way, 1 - core)
+    half = chips // 2
+
+    def turn(step, first, last):
+        ahead = device_at(pos - step * way, core)
+        behind = device_at(pos + step * way, core)
+        sib_ahead = device_at(pos + (step - 1) * way, 1 - core)
+        sib_behind = device_at(pos - (step - 1) * way, 1 - core)
         for j in range(chunks):
-            to_ring(step - 1, owner, j).wait_recv()
-
-            @pl.when(step < chips - 1)
-            def _():
-                to_ring(step, owner, j).start()
-
-            to_sib(step, owner, j).start()
-            to_sib(step - 1, sib_owner, j).wait_recv()
-            out_ref[:, j * wide : (j + 1) * wide] += product(owner, j) + product(sib_owner, j)
+            to_ring(0, step - 1, ahead, j).wait_recv()
+            if not last:
+                to_ring(0, step, ahead, j).start()
+            to_sib(0, step, ahead, j).start()
+            total = product(ahead, j)
+            if not last:
+                to_ring(1, step - 1, behind, j).wait_recv()
+
+                @pl.when(step < half - 1)
+                def _():
+                    to_ring(1, step, behind, j).start()
+
+                to_sib(1, step, behind, j).start()
+                total += product(behind, j)
+            to_sib(0, step - 1, sib_ahead, j).wait_recv()
+            total += product(sib_ahead, j)
+            if not first:
+                to_sib(1, step - 1, sib_behind, j).wait_recv()
+                total += product(sib_behind, j)
+            out_ref[:, j * wide : (j + 1) * wide] += total
+
+    def middle(step, carry):
+        turn(step, False, False)
         return carry
 
-    lax.fori_loop(1, chips, turn, 0)
-
-    last = device_at(pos + (chips - 1) * way, 1 - core)
+    turn(1, True, False)
+    lax.fori_loop(2, half, middle, 0)
+    turn(half, False, True)
+    sib_ahead = device_at(pos + half * way, 1 - core)
     for j in range(chunks):
-        to_sib(chips - 1, last, j).wait_recv()
-        out_ref[:, j * wide : (j + 1) * wide] += product(last, j)
+        to_sib(0, half, sib_ahead, j).wait_recv()
+        out_ref[:, j * wide : (j + 1) * wide] += product(sib_ahead, j)
 
     for d in others:
         halo(d).wait_send()
 
     def settle(step, carry):
         for j in range(chunks):
-            to_sib(step, me, j).wait_send()
-
-            @pl.when(step < chips - 1)
+            to_sib(0, step, me, j).wait_send()
+
+            @pl.when(step < half)
             def _():
-                to_ring(step, me, j).wait_send()
+                to_ring(0, step, me, j).wait_send()
+
+            @pl.when(step < half - 1)
+            def _():
+                to_ring(1, step, me, j).wait_send()
+
+            @pl.when((step > 0) & (step < half))
+            def _():
+                to_sib(1, step, me, j).wait_send()
+
         return carry
 
-    lax.fori_loop(0, chips, settle, 0)
+    lax.fori_loop(0, half + 1, settle, 0)
 
 
 def shards(n, coulomb, chi_tiles, tile_offsets, tile_counts):
@@ -192,27 +229,29 @@
         functools.partial(kernel, n),
         out_shape=jax.ShapeDtypeStruct((tile, nfreq * SLAB), jnp.float32),
         in_specs=[
-            pl.BlockSpec(memory_space=pltpu.SMEM),
-            pl.BlockSpec(memory_space=pltpu.SMEM),
+            pl.BlockSpec(memory_space=pl.ANY),
+            pl.BlockSpec(memory_space=pl.ANY),
             pl.BlockSpec(memory_space=pl.ANY),
             pl.BlockSpec(memory_space=pl.ANY),
         ],
         out_specs=pl.BlockSpec(memory_space=pltpu.VMEM),
         scratch_shapes=[
+            pltpu.SMEM(tile_offsets.shape, jnp.int32),
+            pltpu.SMEM(tile_counts.shape, jnp.int32),
             pltpu.VMEM((tile, points), jnp.bfloat16),
             pltpu.VMEM(chi_tiles.shape[1:], jnp.bfloat16),
             pltpu.VMEM((2 * REACH + 1, SLAB, tile), jnp.bfloat16),
             pltpu.VMEM((n, chunks, tile, 2 * SLAB), jnp.bfloat16),
-            pltpu.SemaphoreType.DMA((2 + chunks,)),
+            pltpu.SemaphoreType.DMA((4 + chunks,)),
             pltpu.SemaphoreType.DMA((2 * REACH + 1,)),
             pltpu.SemaphoreType.DMA((2 * REACH + 1,)),
-            pltpu.SemaphoreType.DMA((chips, chunks)),
-            pltpu.SemaphoreType.DMA((chips, chunks)),
-            pltpu.SemaphoreType.DMA((chips, chunks)),
-            pltpu.SemaphoreType.DMA((chips, chunks)),
+            pltpu.SemaphoreType.DMA((2, chips // 2 + 1, chunks)),
+            pltpu.SemaphoreType.DMA((2, chips // 2 + 1, chunks)),
+            pltpu.SemaphoreType.DMA((2, chips // 2 + 1, chunks)),
+            pltpu.SemaphoreType.DMA((2, chips // 2 + 1, chunks)),
         ],
         compiler_params=pltpu.CompilerParams(
-            collective_id=0, has_side_effects=True, vmem_limit_bytes=48 * 1024 * 1024
+            collective_id=0, has_side_effects=True, vmem_limit_bytes=60 * 1024 * 1024
         ),
         cost_estimate=pl.CostEstimate(
             flops=2 * tile * points * nfreq * SLAB, bytes_accessed=6 * 1024 * 1024, transcendentals=0

time: 40.6 us -> 34.6 us (0.85)
  Pallas kernels: 36.6 us -> 32.1 us
  local copies, waits for them, and re-layouts: 2.99 us -> 1.77 us
    pallas_call x1, Pallas kernels: 36.6 us -> 32.1 us  [shards(): pl.pallas_call(functools.partial(kernel, n), out_shape=jax.ShapeDtypeStru...]
    unnamed x5 -> x1, local copies, waits for them, and re-layouts: 2.99 us -> 1.77 us
where the time goes in v2:
time: 34.6 us; the launch traced here: 34.5 us
  Pallas kernels  32.1 us (93%)
  local copies, waits for them, and re-layouts  1.77 us (5%)
  between operations  0.66 us (2%)
    pallas_call x1, Pallas kernels, shards(): pl.pallas_call(functools.partial(kernel, n), out_shape=jax.ShapeDtypeStru...  32.1 us
    unnamed x1, local copies, waits for them, and re-layouts  1.77 us

profile of v2, /device:TPU:0, one launch (start us, length us, event | category | flops | bytes accessed | tf_op | source)
XLA Modules:
  0.0 34.5 jit_solution(10349544958649581964)
XLA Ops:
  0.7 32.1 %shard_map.46 = f32[256,384]{1,0:T(8,128)} custom-call(s32[1,5]{1,0:T(1,128)} %offsets_hbm.1, s32[1]{0:T(128)S(6)} %copy.6.counts_hbm, bf16[256,4096]{1,0:T(8,128)(2,1)} %coulomb_hbm.1, bf16[1,6,5,256,256]{4,3,2,1,0:T(8,128)(2,1)} %chi_hbm.1), custom_call_target="tpu_custom_call" | custom-call | flops 805306368 | bytes 6291456 | tf_op jit(solution)/shard_map/pallas_call | solution.py:228
  32.7 1.8 %copy.7 = f32[256,384]{1,0:T(8,128)} copy(f32[256,384]{1,0:T(8,128)} %shard_map.46) | data formatting | bytes 786432

commit v3 on v2

--- a/solution.py
+++ b/solution.py
@@ -9,6 +9,7 @@
 
 SLAB = 64
 REACH = 3
+SPLIT = 2
 MESH = pl.DeviceIdType.MESH
 
 
@@ -22,6 +23,7 @@
     chunks = gathered.shape[1]
     per = nfreq // chunks
     wide = per * SLAB
+    pieces = chunks * SPLIT
     chips = n // 2
     cols = 2 if n == 16 else 1
     height = chips // cols
@@ -69,13 +71,10 @@
         c.start()
     rest.start()
 
+    far = 3 * (2 * core - 1)
     barrier = pltpu.get_barrier_semaphore()
-    others = [d for d in range(-REACH, REACH + 1) if d != 0]
-    for d in others:
-        pl.semaphore_signal(
-            barrier, inc=1, device_id={"pts": (me + d + n) % n}, device_id_type=MESH
-        )
-    for peer in (ring_to, ring_from):
+    peers = [sib, (me + 2) % n, (me - 2 + n) % n, (me + far + n) % n, ring_to, ring_from]
+    for peer in peers:
         pl.semaphore_signal(barrier, inc=1, device_id={"pts": peer}, device_id_type=MESH)
 
     first.wait()
@@ -84,25 +83,40 @@
     start = own.astype(jnp.float32)
     out_ref[...] = jnp.concatenate([start] * nfreq, axis=1)
 
-    pl.semaphore_wait(barrier, len(others) + 2)
-
-    def halo(d):
+    pl.semaphore_wait(barrier, len(peers))
+
+    def slab_copy(sem, src, dst, peer):
         return pltpu.make_async_remote_copy(
-            src_ref=slabs.at[REACH],
-            dst_ref=slabs.at[REACH - d],
-            send_sem=halo_send.at[REACH + d],
-            recv_sem=halo_recv.at[REACH - d],
-            device_id={"pts": (me + d + n) % n},
+            src_ref=slabs.at[src],
+            dst_ref=slabs.at[dst],
+            send_sem=halo_send.at[sem],
+            recv_sem=halo_recv.at[sem],
+            device_id={"pts": peer},
             device_id_type=MESH,
         )
 
-    for d in sorted(others, key=abs, reverse=True):
-        halo(d).start()
+    direct = [
+        slab_copy(0, REACH, REACH - far, (me + far + n) % n),
+        slab_copy(1, REACH, REACH - 2, (me + 2) % n),
+        slab_copy(2, REACH, REACH + 2, (me - 2 + n) % n),
+        slab_copy(3, REACH, REACH - 1 + 2 * core, sib),
+    ]
+    passed = [
+        slab_copy(4, REACH - 2, REACH - 3 + 2 * core, sib),
+        slab_copy(5, REACH + 2, REACH + 1 + 2 * core, sib),
+    ]
+    for c in direct:
+        c.start()
+
+    rows = tile // SPLIT
+
+    def piece(owner, i):
+        return gathered.at[owner, i // SPLIT, pl.ds(i % SPLIT * rows, rows)]
 
     def to_ring(stream, step, owner, j):
         return pltpu.make_async_remote_copy(
-            src_ref=gathered.at[owner, j],
-            dst_ref=gathered.at[owner, j],
+            src_ref=piece(owner, j),
+            dst_ref=piece(owner, j),
             send_sem=ring_send.at[stream, step, j],
             recv_sem=ring_recv.at[stream, step, j],
             device_id={"pts": ring_to if stream == 0 else ring_from},
@@ -111,16 +125,20 @@
 
     def to_sib(stream, step, owner, j):
         return pltpu.make_async_remote_copy(
-            src_ref=gathered.at[owner, j],
-            dst_ref=gathered.at[owner, j],
+            src_ref=piece(owner, j),
+            dst_ref=piece(owner, j),
             send_sem=sib_send.at[stream, step, j],
             recv_sem=sib_recv.at[stream, step, j],
             device_id={"pts": sib},
             device_id_type=MESH,
         )
 
-    for d in others:
-        halo(d).wait_recv()
+    direct[1].wait_recv()
+    passed[0].start()
+    direct[2].wait_recv()
+    passed[1].start()
+    for c in (direct[0], direct[3], *passed):
+        c.wait_recv()
 
     for c in table_copies:
         c.wait()
@@ -129,22 +147,25 @@
     for k in range(maxt):
         slab = slabs[offsets_ref[0, k] + REACH]
         picked.append(jnp.where(k < count, slab, jnp.zeros_like(slab)))
-    for j in range(chunks):
-        chi_copies[j].wait()
+    for i in range(pieces):
+        j = i // SPLIT
+        if i % SPLIT == 0:
+            chi_copies[j].wait()
+        band = pl.ds(i % SPLIT * rows, rows)
         parts = []
         for f in range(j * per, (j + 1) * per):
             total = None
             for k in range(maxt):
                 term = lax.dot_general(
-                    chi[f, k], picked[k], (((1,), (1,)), ((), ())),
+                    chi[f, k, band], picked[k], (((1,), (1,)), ((), ())),
                     preferred_element_type=jnp.float32,
                 )
                 total = term if total is None else total + term
             parts.append(total)
-        gathered[me, j] = jnp.concatenate(parts, axis=1).astype(jnp.bfloat16)
-        to_ring(0, 0, me, j).start()
-        to_ring(1, 0, me, j).start()
-        to_sib(0, 0, me, j).start()
+        gathered[me, j, band] = jnp.concatenate(parts, axis=1).astype(jnp.bfloat16)
+        to_ring(0, 0, me, i).start()
+        to_ring(1, 0, me, i).start()
+        to_sib(0, 0, me, i).start()
 
     rest.wait()
 
@@ -162,27 +183,30 @@
         behind = device_at(pos + step * way, core)
         sib_ahead = device_at(pos + (step - 1) * way, 1 - core)
         sib_behind = device_at(pos - (step - 1) * way, 1 - core)
-        for j in range(chunks):
-            to_ring(0, step - 1, ahead, j).wait_recv()
+        for i in range(pieces):
+            to_ring(0, step - 1, ahead, i).wait_recv()
             if not last:
-                to_ring(0, step, ahead, j).start()
-            to_sib(0, step, ahead, j).start()
-            total = product(ahead, j)
+                to_ring(0, step, ahead, i).start()
+            to_sib(0, step, ahead, i).start()
             if not last:
-                to_ring(1, step - 1, behind, j).wait_recv()
+                to_ring(1, step - 1, behind, i).wait_recv()
 
                 @pl.when(step < half - 1)
                 def _():
-                    to_ring(1, step, behind, j).start()
-
-                to_sib(1, step, behind, j).start()
-                total += product(behind, j)
-            to_sib(0, step - 1, sib_ahead, j).wait_recv()
-            total += product(sib_ahead, j)
+                    to_ring(1, step, behind, i).start()
+
+                to_sib(1, step, behind, i).start()
+            to_sib(0, step - 1, sib_ahead, i).wait_recv()
             if not first:
-                to_sib(1, step - 1, sib_behind, j).wait_recv()
-                total += product(sib_behind, j)
-            out_ref[:, j * wide : (j + 1) * wide] += total
+                to_sib(1, step - 1, sib_behind, i).wait_recv()
+            if i % SPLIT == SPLIT - 1:
+                j = i // SPLIT
+                total = product(ahead, j) + product(sib_ahead, j)
+                if not last:
+                    total += product(behind, j)
+                if not first:
+                    total += product(sib_behind, j)
+                out_ref[:, j * wide : (j + 1) * wide] += total
 
     def middle(step, carry):
         turn(step, False, False)
@@ -192,28 +216,30 @@
     lax.fori_loop(2, half, middle, 0)
     turn(half, False, True)
     sib_ahead = device_at(pos + half * way, 1 - core)
-    for j in range(chunks):
-        to_sib(0, half, sib_ahead, j).wait_recv()
-        out_ref[:, j * wide : (j + 1) * wide] += product(sib_ahead, j)
-
-    for d in others:
-        halo(d).wait_send()
+    for i in range(pieces):
+        to_sib(0, half, sib_ahead, i).wait_recv()
+        if i % SPLIT == SPLIT - 1:
+            j = i // SPLIT
+            out_ref[:, j * wide : (j + 1) * wide] += product(sib_ahead, j)
+
+    for c in direct + passed:
+        c.wait_send()
 
     def settle(step, carry):
-        for j in range(chunks):
-            to_sib(0, step, me, j).wait_send()
+        for i in range(pieces):
+            to_sib(0, step, me, i).wait_send()
 
             @pl.when(step < half)
             def _():
-                to_ring(0, step, me, j).wait_send()
+                to_ring(0, step, me, i).wait_send()
 
             @pl.when(step < half - 1)
             def _():
-                to_ring(1, step, me, j).wait_send()
+                to_ring(1, step, me, i).wait_send()
 
             @pl.when((step > 0) & (step < half))
             def _():
-                to_sib(1, step, me, j).wait_send()
+                to_sib(1, step, me, i).wait_send()
 
         return carry
 
@@ -245,10 +271,10 @@
             pltpu.SemaphoreType.DMA((4 + chunks,)),
             pltpu.SemaphoreType.DMA((2 * REACH + 1,)),
             pltpu.SemaphoreType.DMA((2 * REACH + 1,)),
-            pltpu.SemaphoreType.DMA((2, chips // 2 + 1, chunks)),
-            pltpu.SemaphoreType.DMA((2, chips // 2 + 1, chunks)),
-            pltpu.SemaphoreType.DMA((2, chips // 2 + 1, chunks)),
-            pltpu.SemaphoreType.DMA((2, chips // 2 + 1, chunks)),
+            pltpu.SemaphoreType.DMA((2, chips // 2 + 1, chunks * SPLIT)),
+            pltpu.SemaphoreType.DMA((2, chips // 2 + 1, chunks * SPLIT)),
+            pltpu.SemaphoreType.DMA((2, chips // 2 + 1, chunks * SPLIT)),
+            pltpu.SemaphoreType.DMA((2, chips // 2 + 1, chunks * SPLIT)),
         ],
         compiler_params=pltpu.CompilerParams(
             collective_id=0, has_side_effects=True, vmem_limit_bytes=60 * 1024 * 1024

time: 34.6 us -> 33.6 us (0.971)
  Pallas kernels: 32.1 us -> 31 us
    pallas_call x1, Pallas kernels: 32.1 us -> 31 us  [shards(): pl.pallas_call(functools.partial(kernel, n), out_shape=jax.ShapeDtypeStru...]
where the time goes in v3:
time: 33.6 us; the launch traced here: 33.4 us
  Pallas kernels  31 us (92%)
  local copies, waits for them, and re-layouts  1.77 us (5%)
  between operations  0.66 us (2%)
    pallas_call x1, Pallas kernels, shards(): pl.pallas_call(functools.partial(kernel, n), out_shape=jax.ShapeDtypeStru...  31 us
    unnamed x1, local copies, waits for them, and re-layouts  1.77 us

profile of v3, /device:TPU:0, one launch (start us, length us, event | category | flops | bytes accessed | tf_op | source)
XLA Modules:
  0.0 33.4 jit_solution(7511862622263142392)
XLA Ops:
  0.7 31.0 %shard_map.46 = f32[256,384]{1,0:T(8,128)} custom-call(s32[1,5]{1,0:T(1,128)} %offsets_hbm.1, s32[1]{0:T(128)S(6)} %copy.6.counts_hbm, bf16[256,4096]{1,0:T(8,128)(2,1)} %coulomb_hbm.1, bf16[1,6,5,256,256]{4,3,2,1,0:T(8,128)(2,1)} %chi_hbm.1), custom_call_target="tpu_custom_call" | custom-call | flops 805306368 | bytes 6291456 | tf_op jit(solution)/shard_map/pallas_call | solution.py:254
  31.7 1.8 %copy.7 = f32[256,384]{1,0:T(8,128)} copy(f32[256,384]{1,0:T(8,128)} %shard_map.46) | data formatting | bytes 786432

commit v4 on v3

--- a/solution.py
+++ b/solution.py
@@ -16,7 +16,7 @@
 def kernel(
     n, offsets_hbm, counts_hbm, coulomb_hbm, chi_hbm, out_ref,
     offsets_ref, counts_ref, coulomb, chi, slabs, gathered,
-    local_sem, halo_send, halo_recv, ring_send, ring_recv, sib_send, sib_recv,
+    local_sem, halo_send, halo_recv, ring_send, ring_recv, sib_send, sib_recv, end_send, end_recv,
 ):
     tile = coulomb.shape[0]
     nfreq, maxt = chi.shape[:2]
@@ -123,12 +123,22 @@
             device_id_type=MESH,
         )
 
-    def to_sib(stream, step, owner, j):
+    def to_sib(stream, step, owner):
         return pltpu.make_async_remote_copy(
-            src_ref=piece(owner, j),
-            dst_ref=piece(owner, j),
-            send_sem=sib_send.at[stream, step, j],
-            recv_sem=sib_recv.at[stream, step, j],
+            src_ref=gathered.at[owner],
+            dst_ref=gathered.at[owner],
+            send_sem=sib_send.at[stream, step],
+            recv_sem=sib_recv.at[stream, step],
+            device_id={"pts": sib},
+            device_id_type=MESH,
+        )
+
+    def end_to_sib(owner, i):
+        return pltpu.make_async_remote_copy(
+            src_ref=piece(owner, i),
+            dst_ref=piece(owner, i),
+            send_sem=end_send.at[i],
+            recv_sem=end_recv.at[i],
             device_id={"pts": sib},
             device_id_type=MESH,
         )
@@ -165,8 +175,8 @@
         gathered[me, j, band] = jnp.concatenate(parts, axis=1).astype(jnp.bfloat16)
         to_ring(0, 0, me, i).start()
         to_ring(1, 0, me, i).start()
-        to_sib(0, 0, me, i).start()
-
+
+    to_sib(0, 0, me).start()
     rest.wait()
 
     def product(owner, j):
@@ -185,28 +195,34 @@
         sib_behind = device_at(pos - (step - 1) * way, 1 - core)
         for i in range(pieces):
             to_ring(0, step - 1, ahead, i).wait_recv()
-            if not last:
+            if last:
+                end_to_sib(ahead, i).start()
+            else:
                 to_ring(0, step, ahead, i).start()
-            to_sib(0, step, ahead, i).start()
-            if not last:
                 to_ring(1, step - 1, behind, i).wait_recv()
 
                 @pl.when(step < half - 1)
                 def _():
                     to_ring(1, step, behind, i).start()
 
-                to_sib(1, step, behind, i).start()
-            to_sib(0, step - 1, sib_ahead, i).wait_recv()
-            if not first:
-                to_sib(1, step - 1, sib_behind, i).wait_recv()
             if i % SPLIT == SPLIT - 1:
                 j = i // SPLIT
-                total = product(ahead, j) + product(sib_ahead, j)
+                total = product(ahead, j)
                 if not last:
                     total += product(behind, j)
+                out_ref[:, j * wide : (j + 1) * wide] += total
+            if i == pieces - 2:
+                to_sib(0, step - 1, sib_ahead).wait_recv()
                 if not first:
-                    total += product(sib_behind, j)
-                out_ref[:, j * wide : (j + 1) * wide] += total
+                    to_sib(1, step - 1, sib_behind).wait_recv()
+                for j in range(chunks):
+                    total = product(sib_ahead, j)
+                    if not first:
+                        total += product(sib_behind, j)
+                    out_ref[:, j * wide : (j + 1) * wide] += total
+        if not last:
+            to_sib(0, step, ahead).start()
+            to_sib(1, step, behind).start()
 
     def middle(step, carry):
         turn(step, False, False)
@@ -214,36 +230,38 @@
 
     turn(1, True, False)
     lax.fori_loop(2, half, middle, 0)
+    for c in direct + passed:
+        c.wait_send()
+
+    def settle(step, carry):
+        to_sib(0, step, me).wait_send()
+
+        @pl.when(step > 0)
+        def _():
+            to_sib(1, step, me).wait_send()
+
+        for i in range(pieces):
+            to_ring(0, step, me, i).wait_send()
+
+            @pl.when(step < half - 1)
+            def _():
+                to_ring(1, step, me, i).wait_send()
+
+        return carry
+
+    lax.fori_loop(0, half - 1, settle, 0)
     turn(half, False, True)
     sib_ahead = device_at(pos + half * way, 1 - core)
     for i in range(pieces):
-        to_sib(0, half, sib_ahead, i).wait_recv()
+        end_to_sib(sib_ahead, i).wait_recv()
         if i % SPLIT == SPLIT - 1:
             j = i // SPLIT
             out_ref[:, j * wide : (j + 1) * wide] += product(sib_ahead, j)
 
-    for c in direct + passed:
-        c.wait_send()
-
-    def settle(step, carry):
-        for i in range(pieces):
-            to_sib(0, step, me, i).wait_send()
-
-            @pl.when(step < half)
-            def _():
-                to_ring(0, step, me, i).wait_send()
-
-            @pl.when(step < half - 1)
-            def _():
-                to_ring(1, step, me, i).wait_send()
-
-            @pl.when((step > 0) & (step < half))
-            def _():
-                to_sib(1, step, me, i).wait_send()
-
-        return carry
-
-    lax.fori_loop(0, half + 1, settle, 0)
+    for i in range(pieces):
+        end_to_sib(me, i).wait_send()
+
+    settle(half - 1, 0)
 
 
 def shards(n, coulomb, chi_tiles, tile_offsets, tile_counts):
@@ -273,8 +291,10 @@
             pltpu.SemaphoreType.DMA((2 * REACH + 1,)),
             pltpu.SemaphoreType.DMA((2, chips // 2 + 1, chunks * SPLIT)),
             pltpu.SemaphoreType.DMA((2, chips // 2 + 1, chunks * SPLIT)),
-            pltpu.SemaphoreType.DMA((2, chips // 2 + 1, chunks * SPLIT)),
-            pltpu.SemaphoreType.DMA((2, chips // 2 + 1, chunks * SPLIT)),
+            pltpu.SemaphoreType.DMA((2, chips // 2)),
+            pltpu.SemaphoreType.DMA((2, chips // 2)),
+            pltpu.SemaphoreType.DMA((chunks * SPLIT,)),
+            pltpu.SemaphoreType.DMA((chunks * SPLIT,)),
         ],
         compiler_params=pltpu.CompilerParams(
             collective_id=0, has_side_effects=True, vmem_limit_bytes=60 * 1024 * 1024

time: 33.6 us -> 32.9 us (0.979)
  Pallas kernels: 31 us -> 30.4 us
    pallas_call x1, Pallas kernels: 31 us -> 30.4 us  [shards(): pl.pallas_call(functools.partial(kernel, n), out_shape=jax.ShapeDtypeStru...]
where the time goes in v4:
time: 32.9 us; the launch traced here: 32.8 us
  Pallas kernels  30.4 us (92%)
  local copies, waits for them, and re-layouts  1.77 us (5%)
  between operations  0.66 us (2%)
    pallas_call x1, Pallas kernels, shards(): pl.pallas_call(functools.partial(kernel, n), out_shape=jax.ShapeDtypeStru...  30.4 us
    unnamed x1, local copies, waits for them, and re-layouts  1.77 us

profile of v4, /device:TPU:0, one launch (start us, length us, event | category | flops | bytes accessed | tf_op | source)
XLA Modules:
  0.0 32.8 jit_solution(10116418604110773894)
XLA Ops:
  0.7 30.4 %shard_map.46 = f32[256,384]{1,0:T(8,128)} custom-call(s32[1,5]{1,0:T(1,128)} %offsets_hbm.1, s32[1]{0:T(128)S(6)} %copy.6.counts_hbm, bf16[256,4096]{1,0:T(8,128)(2,1)} %coulomb_hbm.1, bf16[1,6,5,256,256]{4,3,2,1,0:T(8,128)(2,1)} %chi_hbm.1), custom_call_target="tpu_custom_call" | custom-call | flops 805306368 | bytes 6291456 | tf_op jit(solution)/shard_map/pallas_call | solution.py:272
  31.0 1.8 %copy.7 = f32[256,384]{1,0:T(8,128)} copy(f32[256,384]{1,0:T(8,128)} %shard_map.46) | data formatting | bytes 786432

commit v5 on v4

--- a/solution.py
+++ b/solution.py
@@ -9,7 +9,7 @@
 
 SLAB = 64
 REACH = 3
-SPLIT = 2
+SPLIT = 4
 MESH = pl.DeviceIdType.MESH
 
 
@@ -267,7 +267,7 @@
 def shards(n, coulomb, chi_tiles, tile_offsets, tile_counts):
     tile, points = coulomb.shape
     _, nfreq, maxt = chi_tiles.shape[:3]
-    chunks = nfreq // 2
+    chunks = 1
     chips = n // 2
     return pl.pallas_call(
         functools.partial(kernel, n),
@@ -285,7 +285,7 @@
             pltpu.VMEM((tile, points), jnp.bfloat16),
             pltpu.VMEM(chi_tiles.shape[1:], jnp.bfloat16),
             pltpu.VMEM((2 * REACH + 1, SLAB, tile), jnp.bfloat16),
-            pltpu.VMEM((n, chunks, tile, 2 * SLAB), jnp.bfloat16),
+            pltpu.VMEM((n, chunks, tile, nfreq // chunks * SLAB), jnp.bfloat16),
             pltpu.SemaphoreType.DMA((4 + chunks,)),
             pltpu.SemaphoreType.DMA((2 * REACH + 1,)),
             pltpu.SemaphoreType.DMA((2 * REACH + 1,)),

time: 32.9 us -> 32.7 us (level)
  Pallas kernels: 30.4 us -> 30 us
where the time goes in v5:
time: 32.7 us; the launch traced here: 32.5 us
  Pallas kernels  30 us (92%)
  local copies, waits for them, and re-layouts  1.77 us (5%)
  between operations  0.66 us (2%)
    pallas_call x1, Pallas kernels, shards(): pl.pallas_call(functools.partial(kernel, n), out_shape=jax.ShapeDtypeStru...  30 us
    unnamed x1, local copies, waits for them, and re-layouts  1.77 us

profile of v5, /device:TPU:0, one launch (start us, length us, event | category | flops | bytes accessed | tf_op | source)
XLA Modules:
  0.0 32.5 jit_solution(423284219342179890)
XLA Ops:
  0.7 30.0 %shard_map.46 = f32[256,384]{1,0:T(8,128)} custom-call(s32[1,5]{1,0:T(1,128)} %offsets_hbm.1, s32[1]{0:T(128)S(6)} %copy.6.counts_hbm, bf16[256,4096]{1,0:T(8,128)(2,1)} %coulomb_hbm.1, bf16[1,6,5,256,256]{4,3,2,1,0:T(8,128)(2,1)} %chi_hbm.1), custom_call_target="tpu_custom_call" | custom-call | flops 805306368 | bytes 6291456 | tf_op jit(solution)/shard_map/pallas_call | solution.py:272
  30.7 1.8 %copy.7 = f32[256,384]{1,0:T(8,128)} copy(f32[256,384]{1,0:T(8,128)} %shard_map.46) | data formatting | bytes 786432

commit v6 on v5

--- a/solution.py
+++ b/solution.py
@@ -183,9 +183,6 @@
         columns = pl.ds(pl.multiple_of(owner * tile, tile), tile)
         return jnp.dot(coulomb[:, columns], gathered[owner, j], preferred_element_type=jnp.float32)
 
-    for j in range(chunks):
-        out_ref[:, j * wide : (j + 1) * wide] += product(me, j)
-
     half = chips // 2
 
     def turn(step, first, last):
@@ -217,6 +214,8 @@
                     to_sib(1, step - 1, sib_behind).wait_recv()
                 for j in range(chunks):
                     total = product(sib_ahead, j)
+                    if first:
+                        total += product(me, j)
                     if not first:
                         total += product(sib_behind, j)
                     out_ref[:, j * wide : (j + 1) * wide] += total

time: 32.7 us -> 32.7 us (level)
  no operation moved by 1% of the time
where the time goes in v6:
time: 32.7 us; the launch traced here: 32.5 us
  Pallas kernels  30 us (92%)
  local copies, waits for them, and re-layouts  1.77 us (5%)
  between operations  0.66 us (2%)
    pallas_call x1, Pallas kernels, shards(): pl.pallas_call(functools.partial(kernel, n), out_shape=jax.ShapeDtypeStru...  30 us
    unnamed x1, local copies, waits for them, and re-layouts  1.77 us

profile of v6, /device:TPU:0, one launch (start us, length us, event | category | flops | bytes accessed | tf_op | source)
XLA Modules:
  0.0 32.5 jit_solution(1755024655597461295)
XLA Ops:
  0.7 30.0 %shard_map.46 = f32[256,384]{1,0:T(8,128)} custom-call(s32[1,5]{1,0:T(1,128)} %offsets_hbm.1, s32[1]{0:T(128)S(6)} %copy.6.counts_hbm, bf16[256,4096]{1,0:T(8,128)(2,1)} %coulomb_hbm.1, bf16[1,6,5,256,256]{4,3,2,1,0:T(8,128)(2,1)} %chi_hbm.1), custom_call_target="tpu_custom_call" | custom-call | flops 805306368 | bytes 6291456 | tf_op jit(solution)/shard_map/pallas_call | solution.py:271
  30.7 1.8 %copy.7 = f32[256,384]{1,0:T(8,128)} copy(f32[256,384]{1,0:T(8,128)} %shard_map.46) | data formatting | bytes 786432
